TPU v7x, 32 devices: a whole 2x2x4 slice. The times are simulated.
32 devices in a mesh: slides: 2 (over y), seq: 16 (over z, x, core), mp: 1.
Axes of the slice: x: 2, y: 2, z: 4, core: 2. Of those that a mesh axis runs over, the one named last changes fastest.
Arguments:
- tokens: bfloat16 [32768, 768], P(('slides', 'seq', 'mp')), parts along dimension 0, may hold values from -6 to 6
- attn_gain: float32 [768], replicated, may hold values from 0.25 to 1.75
- query_first: bfloat16 [768, 768], P(None, 'mp'), may hold values from -4 to 4
- key_first: bfloat16 [768, 768], P(None, 'mp'), may hold values from -4 to 4
- segment_value: bfloat16 [768, 768], P(None, 'mp'), may hold values from -0.21875 to 0.21875
- output_first: bfloat16 [768, 768], P('mp'), may hold values from -0.875 to 0.875
- mlp_gain: float32 [768], replicated, may hold values from 0.25 to 1.75
- up_weight: bfloat16 [768, 3072], P(None, 'mp'), may hold values from -0.21875 to 0.21875
- down_weight: bfloat16 [3072, 768], P('mp'), may hold values from -0.109375 to 0.109375
- second_gain: float32 [768], replicated, may hold values from 0.25 to 1.75
- query_second: bfloat16 [768, 768], P(None, 'mp'), may hold values from -4 to 4
- key_second: bfloat16 [768, 768], P(None, 'mp'), may hold values from -4 to 4
- value_second: bfloat16 [768, 768], P(None, 'mp'), may hold values from -0.21875 to 0.21875
- output_second: bfloat16 [768, 768], P('mp'), may hold values from -0.875 to 0.875
- segment_offset: int32 [16], P('mp'), may hold values from 0 to 63
- global_offset: int32 [16], P('mp'), may hold values from 0 to 63
Outputs:
- encoded: bfloat16 [32768, 768], P(('slides', 'seq', 'mp')), parts along dimension 0
There are 2 independent parts, one for each index of `slides`. A program takes and returns all parts, laid end to end along the dimension named above; an argument that names none is the same for every part. Nothing has to cross between parts.
All inputs are finite; a program needn't handle non-finite values.
Results may differ from a plain program's by a relative error of at most 0.03.
The roundings to bfloat16 on the way count: a program that leaves them out, or rounds other values in their place, can miss the bound.
Values may be sent and summed in bfloat16 or wider, within the bound.
No kernel may reach another device: no remote copies, remote signals or barrier semaphores. Data moves between devices by JAX's collectives and lax.ppermute only.
A program may use at most 128 MiB of HBM per device.

v0:
```python
import jax
import jax.numpy as jnp
from jax import lax
from jax.sharding import PartitionSpec as P

KEYS = 256
SEG_MAX = 16


def swapped(x, axis, apart):
    return lax.ppermute(x, axis, [(i, i ^ 1 << apart) for i in range(lax.axis_size(axis))])


def norm_rows(values, gain):
    center = values - jnp.mean(values, axis=-1, keepdims=True)
    spread = jnp.mean(center * center, axis=-1, keepdims=True)
    return (center * lax.rsqrt(spread + 1e-05) * gain).astype(jnp.bfloat16)


def pick_keys(hidden, offsets, stride, key_weight, value_weight):
    token_count, width = hidden.shape
    head_count = offsets.shape[0]
    head_size = key_weight.shape[1] // head_count
    grouped_rows = hidden.reshape(token_count // stride, stride, width)
    dilation_selector = (
        lax.broadcasted_iota(jnp.int32, (stride, head_count), 0) == offsets[None, :]
    ).astype(jnp.bfloat16)
    chosen = jnp.einsum(
        "nof,oj->njf", grouped_rows, dilation_selector, preferred_element_type=jnp.float32
    ).astype(jnp.bfloat16)
    key_heads = jnp.einsum(
        "xkr,rkf->xkf",
        chosen,
        key_weight.reshape(width, head_count, head_size),
        preferred_element_type=jnp.float32,
    ).astype(jnp.bfloat16)
    value_heads = jnp.einsum(
        "xkr,rkf->xkf",
        chosen,
        value_weight.reshape(width, head_count, head_size),
        preferred_element_type=jnp.float32,
    ).astype(jnp.bfloat16)
    picked = token_count // stride
    return jnp.stack(
        [
            key_heads.reshape(picked, head_count * head_size),
            value_heads.reshape(picked, head_count * head_size),
        ]
    )


def attend_local(query, keyval, head_count):
    token_count, width = query.shape
    head_size = width // head_count
    query_heads = query.reshape(token_count, head_count, head_size)
    key_heads = keyval[0].reshape(-1, head_count, head_size)
    value_heads = keyval[1].reshape(-1, head_count, head_size)
    scores = jnp.einsum(
        "thd,khd->htk", query_heads, key_heads, preferred_element_type=jnp.float32
    ) * head_size ** (-0.5)
    highest = jnp.max(scores, axis=-1, keepdims=True)
    weights = jnp.exp(scores - highest)
    weights = (weights / jnp.sum(weights, axis=-1, keepdims=True)).astype(jnp.bfloat16)
    mixed = jnp.einsum(
        "htk,khd->thd", weights, value_heads, preferred_element_type=jnp.float32
    ).astype(jnp.bfloat16)
    return mixed.reshape(token_count, width)


def merge_branch_pair(mine, other, level, token_position):
    lower = token_position >> level & 1 == 0
    return jnp.where(
        lower, jnp.concatenate((mine, other), axis=1), jnp.concatenate((other, mine), axis=1)
    )


def spread_segment(keyval, seg_span, token_position):
    for level in range(seg_span.bit_length() - 1):
        partner = swapped(keyval, "seq", level)
        keyval = merge_branch_pair(keyval, partner, level, token_position)
    return keyval


def spread_global(keyval_two):
    keyval_two = lax.all_gather(keyval_two, "seq", axis=1, tiled=True)
    return keyval_two


def combine(partial_value, residual_full, need_full):
    row_count = residual_full.shape[0] // lax.axis_size("mp")
    row_start = lax.axis_index("mp") * row_count
    share = lax.psum_scatter(partial_value, "mp", scatter_dimension=0, tiled=True)
    own_rows = lax.dynamic_slice_in_dim(residual_full, row_start, row_count, 0)
    own_rows = (own_rows.astype(jnp.float32) + share).astype(jnp.bfloat16)
    full_rows = lax.all_gather(own_rows, "mp", axis=0, tiled=True) if need_full else own_rows
    return (own_rows, full_rows)


def body(
    tokens,
    attn_gain,
    query_first,
    key_first,
    segment_value,
    output_first,
    mlp_gain,
    up_weight,
    down_weight,
    second_gain,
    query_second,
    key_second,
    value_second,
    output_second,
    segment_offset,
    global_offset,
):
    seq_count = lax.axis_size("seq")
    token_position = lax.axis_index("seq")
    seg_span = min(SEG_MAX, seq_count)
    head_count = segment_offset.shape[0]
    full_rows = lax.all_gather(tokens, "mp", axis=0, tiled=True)
    token_count = full_rows.shape[0]
    hidden = norm_rows(full_rows.astype(jnp.float32), attn_gain)
    query = jnp.dot(hidden, query_first, preferred_element_type=jnp.float32).astype(jnp.bfloat16)
    seg_stride = token_count // (KEYS // seg_span)
    keyval = pick_keys(hidden, segment_offset, seg_stride, key_first, segment_value)
    keyval = spread_segment(keyval, seg_span, token_position)
    mixed = attend_local(query, keyval, head_count)
    partial_value = jnp.dot(mixed, output_first, preferred_element_type=jnp.float32)
    own_rows, first_rows = combine(partial_value, full_rows, True)
    normed = norm_rows(first_rows.astype(jnp.float32), mlp_gain)
    inner = jax.nn.gelu(
        jnp.dot(normed, up_weight, preferred_element_type=jnp.float32), approximate=True
    ).astype(jnp.bfloat16)
    partial_value = jnp.dot(inner, down_weight, preferred_element_type=jnp.float32)
    own_rows, second_rows = combine(partial_value, first_rows, True)
    hidden_two = norm_rows(second_rows.astype(jnp.float32), second_gain)
    query_two = jnp.dot(hidden_two, query_second, preferred_element_type=jnp.float32).astype(
        jnp.bfloat16
    )
    glob_stride = token_count // (KEYS // seq_count)
    keyval_two = pick_keys(hidden_two, global_offset, glob_stride, key_second, value_second)
    keyval_two = spread_global(keyval_two)
    mixed_two = attend_local(query_two, keyval_two, head_count)
    partial_value = jnp.dot(mixed_two, output_second, preferred_element_type=jnp.float32)
    own_rows, unused_rows = combine(partial_value, second_rows, False)
    return own_rows


def solution(mesh):
    placed = (
        P(("slides", "seq", "mp"), None),
        P(),
        P(None, "mp"),
        P(None, "mp"),
        P(None, "mp"),
        P("mp", None),
        P(),
        P(None, "mp"),
        P("mp", None),
        P(),
        P(None, "mp"),
        P(None, "mp"),
        P(None, "mp"),
        P("mp", None),
        P("mp"),
        P("mp"),
    )
    return jax.shard_map(
        body,
        mesh=mesh,
        in_specs=placed,
        out_specs=P(("slides", "seq", "mp"), None),
        check_vma=False,
    )
```

profile of v0, /device:TPU:1, one launch (start us, length us, event | category | flops | bytes accessed | tf_op | source)
XLA Modules:
  0.0 132.8 jit_solution(15052510869012871012)
XLA Ops:
  0.0 2.5 %copy.27 = bf16[768,768]{0,1:T(8,128)(2,1)} copy(bf16[768,768]{1,0:T(8,128)(2,1)} %param.19) | data formatting | bytes 2359296 | tf_op args[3]
  2.8 0.6 fusion.34
  3.5 0.5 fusion.36
  4.0 1.1 copy-done.3
  5.5 0.4 fusion.62
  6.1 2.4 %copy.30 = bf16[768,768]{0,1:T(8,128)(2,1)} copy(bf16[768,768]{1,0:T(8,128)(2,1)} %param.20) | data formatting | bytes 2359296 | tf_op args[4]
  8.5 1.7 %fusion.63 = bf16[16,16,48]{2,0,1:T(8,128)(2,1)S(1)} fusion(bf16[768,16,48]{0,2,1:T(8,128)(2,1)} %bitcast.67, bf16[16,16,768]{2,1,0:T(8,128)(2,1)S(1)} %fusion.60), kind=kOutput, calls=%fused_computation.70 | convolution fusion | flops 18886656 | bytes 1597440 | tf_op jit(solution)/shard_map/xkr,rkf->xkf/dot_general | solution.py:37
  10.5 1.2 collective-permute-done
  11.7 2.4 %collective-permute-start.1 = (bf16[2,32,768]{2,1,0:T(8,128)(2,1)S(1)}, bf16[2,32,768]{2,1,0:T(8,128)(2,1)S(1)}, u32[]{:S(2)}, u32[]{:S(2)}) collective-permute-start(bf16[2,32,768]{2,1,0:T(8,128)(2,1)S(1)} %maximum_select_fusion.3), channel_id=1, source_target_pairs={{0,2},{1,3},{2,0},{3,1},{4,6},{5,7},{6,4},{7,5},{8,10},{9,11},{10,... | collective-permute-start | bytes 294920 | tf_op jit(solution)/shard_map/ppermute | solution.py:11
  14.1 2.9 %collective-permute-done.1 = bf16[2,32,768]{2,1,0:T(8,128)(2,1)S(1)} collective-permute-done((bf16[2,32,768]{2,1,0:T(8,128)(2,1)S(1)}, bf16[2,32,768]{2,1,0:T(8,128)(2,1)S(1)}, u32[]{:S(2)}, u32[]{:S(2)}) %collective-permute-start.1) | collective-permute-done | bytes 98336 | tf_op jit(solution)/shard_map/ppermute | solution.py:11
  17.0 1.3 collective-permute-start.2
  18.3 4.3 %collective-permute-done.2 = bf16[2,64,768]{2,1,0:T(8,128)(2,1)S(1)} collective-permute-done((bf16[2,64,768]{2,1,0:T(8,128)(2,1)S(1)}, bf16[2,64,768]{2,1,0:T(8,128)(2,1)S(1)}, u32[]{:S(2)}, u32[]{:S(2)}) %collective-permute-start.2) | collective-permute-done | bytes 196640 | tf_op jit(solution)/shard_map/ppermute | solution.py:11
  22.7 2.0 %collective-permute-start.3 = (bf16[2,128,768]{2,1,0:T(8,128)(2,1)S(1)}, bf16[2,128,768]{2,1,0:T(8,128)(2,1)S(1)}, u32[]{:S(2)}, u32[]{:S(2)}) collective-permute-start(bf16[2,128,768]{2,1,0:T(8,128)(2,1)S(1)} %maximum_select_fusion.1), channel_id=1, source_target_pairs={{0,8},{1,9},{2,10},{3,11},{4,12},{5,13},{6,14},{7,15},{8,0},{9,1},... | collective-permute-start | bytes 1179656 | tf_op jit(solution)/shard_map/ppermute | solution.py:11
  24.7 2.4 %copy.39 = bf16[768,768]{0,1:T(8,128)(2,1)} copy(bf16[768,768]{1,0:T(8,128)(2,1)} %param.28) | data formatting | bytes 2359296 | tf_op args[12]
  27.1 2.4 %copy.36 = bf16[768,768]{0,1:T(8,128)(2,1)} copy(bf16[768,768]{1,0:T(8,128)(2,1)} %param.27) | data formatting | bytes 2359296 | tf_op args[11]
  29.5 4.3 %convolution_convert_fusion.1 = bf16[1024,768]{0,1:T(8,128)(2,1)} fusion(bf16[1024,768]{1,0:T(8,128)(2,1)} %copy-done.3, bf16[768,768]{1,0:T(8,128)(2,1)} %param.18), kind=kOutput, calls=%fused_computation.57 | convolution fusion | flops 1208745984 | bytes 4325376 | tf_op jit(solution)/shard_map/dot_general | solution.py:124
  33.8 8.7 %collective-permute-done.3 = bf16[2,128,768]{2,1,0:T(8,128)(2,1)S(1)} collective-permute-done((bf16[2,128,768]{2,1,0:T(8,128)(2,1)S(1)}, bf16[2,128,768]{2,1,0:T(8,128)(2,1)S(1)}, u32[]{:S(2)}, u32[]{:S(2)}) %collective-permute-start.3) | collective-permute-done | bytes 393248 | tf_op jit(solution)/shard_map/ppermute | solution.py:11
  42.9 0.9 copy.33
  44.0 10.4 %fusion.84 = (f32[16,1024]{1,0:T(8,128)}, f32[16,1024,256]{1,2,0:T(8,128)}) fusion(bf16[1024,16,48]{0,2,1:T(8,128)(2,1)} %bitcast.72, bf16[256,16,48]{0,2,1:T(8,128)(2,1)S(1)} %bitcast.70), kind=kOutput, calls=%fused_computation.104 | convolution fusion | flops 415236352 | bytes 18808832 | tf_op jit(solution)/shard_map/sub | solution.py:62
  54.3 7.3 %fusion.47 = bf16[16,48,1024]{2,1,0:T(8,128)(2,1)S(1)} fusion(bf16[256,16,48]{0,2,1:T(8,128)(2,1)S(1)} %bitcast.69, f32[16,1024,256]{1,2,0:T(8,128)} %get-tuple-element.10, f32[16,1024]{1,0:T(8,128)} %get-tuple-element.9), kind=kOutput, calls=%fused_computation.55 | convolution fusion | flops 411828224 | bytes 18808832 | tf_op jit(solution)/shard_map/htk,khd->thd/dot_general | solution.py:64
  61.7 1.6 %convert_reduce_fusion.1 = (f32[1024]{0:T(1024)S(1)}, bf16[1024,768]{1,0:T(8,128)(2,1)S(1)}) fusion(bf16[1024,768]{0,1:T(8,128)(2,1)S(1)} %bitcast.74, bf16[768,768]{1,0:T(8,128)(2,1)S(1)} %copy-done, bf16[1024,768]{1,0:T(8,128)(2,1)S(1)} %copy-done.2), kind=kOutput, calls=%fused_computation.29 | convolution fusion | flops 1211890688 | bytes 5902336 | tf_op jit(solution)/shard_map/dot_general | solution.py:129
  63.3 0.6 fusion.31
  63.9 0.5 copy-done.8
  64.4 15.5 %convert_reduce_fusion = (f32[1024]{0:T(1024)S(1)}, bf16[1024,768]{1,0:T(8,128)(2,1)S(1)}) fusion(bf16[3072,768]{1,0:T(8,128)(2,1)} %param.24, bf16[768,3072]{1,0:T(8,128)(2,1)} %param.23, bf16[1024,768]{1,0:T(8,128)(2,1)} %copy-done.8, f32[768]{0:T(1024)S(1)} %copy-done.15, f32[1024]{0:T(1024)S(1)} %add_rsqrt_fusion.1, f32[1024]{0:T(1024)S(1)} %broadcast_multiply_fusion.1), kind=kOutput, calls=%fused_computation.26 | convolution fusion | flops 9699851264 | bytes 12598272 | tf_op jit(solution)/shard_map/dot_general | solution.py:135
  79.9 0.6 fusion.28
  80.6 0.5 fusion.30
  81.1 1.1 copy-done.4
  83.8 24.5 %all_gather.2 = bf16[2,256,768]{2,1,0:T(8,128)(2,1)S(1)} all-gather(bf16[2,16,768]{2,1,0:T(8,128)(2,1)S(1)} %pad_maximum_fusion), channel_id=1, replica_groups=mesh['slides'=2,'seq'=16,'mp'=1] {'seq'}, dimensions={1}, use_global_device_ids=true | all-gather | bytes 835584 | tf_op jit(solution)/shard_map/all_gather | solution.py:85
  108.5 4.3 %convolution_convert_fusion = bf16[1024,768]{0,1:T(8,128)(2,1)} fusion(bf16[1024,768]{1,0:T(8,128)(2,1)} %copy-done.4, bf16[768,768]{1,0:T(8,128)(2,1)} %param.26), kind=kOutput, calls=%fused_computation.56 | convolution fusion | flops 1208745984 | bytes 4325376 | tf_op jit(solution)/shard_map/dot_general | solution.py:138
  113.0 9.7 %fusion.87 = (f32[16,1024]{1,0:T(8,128)S(1)}, f32[16,1024,256]{1,2,0:T(8,128)}) fusion(bf16[1024,16,48]{0,2,1:T(8,128)(2,1)} %bitcast.73, bf16[256,16,48]{0,2,1:T(8,128)(2,1)S(1)} %bitcast.71), kind=kOutput, calls=%fused_computation.105 | convolution fusion | flops 415236352 | bytes 18808832 | tf_op jit(solution)/shard_map/sub | solution.py:62
  122.8 7.4 %fusion.46 = bf16[16,48,1024]{2,1,0:T(8,128)(2,1)S(1)} fusion(bf16[256,16,48]{0,2,1:T(8,128)(2,1)S(1)} %bitcast.68, f32[16,1024,256]{1,2,0:T(8,128)} %get-tuple-element.16, f32[16,1024]{1,0:T(8,128)S(1)} %get-tuple-element.15), kind=kOutput, calls=%fused_computation.54 | convolution fusion | flops 411828224 | bytes 18808832 | tf_op jit(solution)/shard_map/htk,khd->thd/dot_general | solution.py:64
  130.2 2.6 %fusion.39 = bf16[1024,768]{1,0:T(8,128)(2,1)} fusion(bf16[1024,768]{1,0:T(8,128)(2,1)S(1)} %get-tuple-element.14, bf16[1024,768]{0,1:T(8,128)(2,1)S(1)} %bitcast.75, bf16[768,768]{1,0:T(8,128)(2,1)S(1)} %copy-done.14), kind=kOutput, calls=%fused_computation.50 | convolution fusion | flops 1210318848 | bytes 5898240 | tf_op jit(solution)/shard_map/dot_general | solution.py:145
  (61 shorter events, 3.7 us)
Async XLA Ops:
  0.0 61.7 %copy-start = (bf16[768,768]{1,0:T(8,128)(2,1)S(1)}, bf16[768,768]{1,0:T(8,128)(2,1)}, u32[]{:S(2)}) copy-start(bf16[768,768]{1,0:T(8,128)(2,1)} %param.21) | copy-start | bytes 3538948
  0.0 2.5 %copy-start.2 = (bf16[1024,768]{1,0:T(8,128)(2,1)S(1)}, bf16[1024,768]{1,0:T(8,128)(2,1)}, u32[]{:S(2)}) copy-start(bf16[1024,768]{1,0:T(8,128)(2,1)} %param.16) | copy-start | bytes 4718596
  0.0 3.5 %copy-start.10 = (f32[768]{0:T(1024)S(1)}, f32[768]{0:T(1024)}, u32[]{:S(2)}) copy-start(f32[768]{0:T(1024)} %param.17) | copy-start | bytes 9220
  2.5 2.6 %copy-start.12 = (s32[16]{0:T(128)S(1)}, s32[16]{0:T(128)}, u32[]{:S(2)}) copy-start(s32[16]{0:T(128)} %param.30) | copy-start | bytes 196
  2.8 2.7 %copy-start.7 = (bf16[768,768]{0,1:T(8,128)(2,1)S(1)}, bf16[768,768]{0,1:T(8,128)(2,1)}, u32[]{:S(2)}) copy-start(bf16[768,768]{0,1:T(8,128)(2,1)} %copy.27) | copy-start | bytes 3538948
  4.0 1.1 copy-start.3
  10.3 1.3 collective-permute-start
  11.7 5.3 %collective-permute-start.1 = (bf16[2,32,768]{2,1,0:T(8,128)(2,1)S(1)}, bf16[2,32,768]{2,1,0:T(8,128)(2,1)S(1)}, u32[]{:S(2)}, u32[]{:S(2)}) collective-permute-start(bf16[2,32,768]{2,1,0:T(8,128)(2,1)S(1)} %maximum_select_fusion.3), channel_id=1, source_target_pairs={{0,2},{1,3},{2,0},{3,1},{4,6},{5,7},{6,4},{7,5},{8,10},{9,11},{10,... | collective-permute-start | bytes 294920 | tf_op jit(solution)/shard_map/ppermute | solution.py:11
  17.0 5.6 %collective-permute-start.2 = (bf16[2,64,768]{2,1,0:T(8,128)(2,1)S(1)}, bf16[2,64,768]{2,1,0:T(8,128)(2,1)S(1)}, u32[]{:S(2)}, u32[]{:S(2)}) collective-permute-start(bf16[2,64,768]{2,1,0:T(8,128)(2,1)S(1)} %maximum_select_fusion.2), channel_id=1, source_target_pairs={{0,4},{1,5},{2,6},{3,7},{4,0},{5,1},{6,2},{7,3},{8,12},{9,13},{10,... | collective-permute-start | bytes 589832 | tf_op jit(solution)/shard_map/ppermute | solution.py:11
  22.7 19.8 %collective-permute-start.3 = (bf16[2,128,768]{2,1,0:T(8,128)(2,1)S(1)}, bf16[2,128,768]{2,1,0:T(8,128)(2,1)S(1)}, u32[]{:S(2)}, u32[]{:S(2)}) collective-permute-start(bf16[2,128,768]{2,1,0:T(8,128)(2,1)S(1)} %maximum_select_fusion.1), channel_id=1, source_target_pairs={{0,8},{1,9},{2,10},{3,11},{4,12},{5,13},{6,14},{7,15},{8,0},{9,1},... | collective-permute-start | bytes 1179656 | tf_op jit(solution)/shard_map/ppermute | solution.py:11
  44.0 10.4 %copy-start.9 = (bf16[1,256,768]{1,2,0:T(8,128)(2,1)S(1)}, bf16[1,256,768]{1,2,0:T(8,128)(2,1)}, u32[]{:S(2)}) copy-start(bf16[1,256,768]{1,2,0:T(8,128)(2,1)} %copy.33) | copy-start | bytes 1179652
  61.7 2.7 %copy-start.15 = (f32[768]{0:T(1024)S(1)}, f32[768]{0:T(1024)}, u32[]{:S(2)}) copy-start(f32[768]{0:T(1024)} %param.22) | copy-start | bytes 9220
  63.3 1.1 copy-start.8
  64.4 16.1 %copy-start.11 = (f32[768]{0:T(1024)S(1)}, f32[768]{0:T(1024)}, u32[]{:S(2)}) copy-start(f32[768]{0:T(1024)} %param.25) | copy-start | bytes 9220
  79.9 2.4 %copy-start.13 = (s32[16]{0:T(128)S(1)}, s32[16]{0:T(128)}, u32[]{:S(2)}) copy-start(s32[16]{0:T(128)} %param.31) | copy-start | bytes 196
  79.9 2.7 %copy-start.6 = (bf16[768,768]{0,1:T(8,128)(2,1)S(1)}, bf16[768,768]{0,1:T(8,128)(2,1)}, u32[]{:S(2)}) copy-start(bf16[768,768]{0,1:T(8,128)(2,1)} %copy.39) | copy-start | bytes 3538948
  80.6 2.7 %copy-start.5 = (bf16[768,768]{0,1:T(8,128)(2,1)S(1)}, bf16[768,768]{0,1:T(8,128)(2,1)}, u32[]{:S(2)}) copy-start(bf16[768,768]{0,1:T(8,128)(2,1)} %copy.36) | copy-start | bytes 3538948
  81.1 1.1 copy-start.4
  122.7 7.5 %copy-start.14 = (bf16[768,768]{1,0:T(8,128)(2,1)S(1)}, bf16[768,768]{1,0:T(8,128)(2,1)}, u32[]{:S(2)}) copy-start(bf16[768,768]{1,0:T(8,128)(2,1)} %param.29) | copy-start | bytes 3538948
  130.2 2.6 %copy-start.1 = (bf16[768,768]{1,0:T(8,128)(2,1)S(1)}, bf16[768,768]{1,0:T(8,128)(2,1)}, u32[]{:S(2)}) copy-start(bf16[768,768]{1,0:T(8,128)(2,1)} %param.21) | copy-start | bytes 3538948
where the time goes:
time: 133 us
  matrix products  66.8 us (50%)
  blocking collectives  24.5 us (18%)
  waiting for transfers between devices  17.1 us (13%)
  local copies, waits for them, and re-layouts  14.6 us (11%)
  starting transfers between devices  5.8 us (4%)
  other arithmetic  3.63 us (3%)
    all_gather x1, blocking collectives, spread_global(): keyval_two = lax.all_gather(keyval_two, 'seq', axis=1, tiled=True)  24.5 us
    sub x2, matrix products, attend_local(): weights = jnp.exp(scores - highest)  20.1 us
    ppermute x4, waiting for transfers between devices, swapped(): lax.ppermute(x, axis, [(i, i ^ 1 << apart) for i in range(lax.axis_size(a...  17.1 us
    dot_general x1, matrix products, body(): jnp.dot(inner, down_weight, preferred_element_type=jnp.float32)  15.5 us
    dot_general x2, matrix products, attend_local(): jnp.einsum('htk,khd->thd', weights, value_heads, preferred_element_type=j...  14.8 us
    unnamed x37, local copies, waits for them, and re-layouts  12.5 us
    ppermute x4, starting transfers between devices, swapped(): lax.ppermute(x, axis, [(i, i ^ 1 << apart) for i in range(lax.axis_size(a...  5.8 us
    dot_general x1, matrix products, body(): jnp.dot(hidden_two, query_second, preferred_element_type=jnp.float32)  4.34 us
  transfers between devices with their start and end apart: 4, of which 4 were waited for; matrix products, arithmetic and copies ran while one was open for 7% of the time, Pallas kernels for 0%

commit v1 on v0

--- a/solution.py
+++ b/solution.py
@@ -1,10 +1,20 @@
+import functools
+import math
+
 import jax
 import jax.numpy as jnp
 from jax import lax
+from jax.experimental import pallas as pl
+from jax.experimental.pallas import tpu as pltpu
 from jax.sharding import PartitionSpec as P
 
 KEYS = 256
 SEG_MAX = 16
+ROWS = 256
+LOG2E = 1.4426950408889634
+BF16 = jnp.bfloat16
+F32 = jnp.float32
+VMEM_LIMIT = 22 * 1024 * 1024
 
 
 def swapped(x, axis, apart):
@@ -96,7 +106,7 @@
     return (own_rows, full_rows)
 
 
-def body(
+def split_body(
     tokens,
     attn_gain,
     query_first,
@@ -147,6 +157,643 @@
     return own_rows
 
 
+def one_hot(condition):
+    return jnp.where(condition, 1.0, 0.0).astype(BF16)
+
+
+def dot(left, right):
+    return jnp.dot(left, right, preferred_element_type=F32)
+
+
+def pieces(count, size):
+    size = size if count % size == 0 else count
+    return [slice(start, start + size) for start in range(0, count, size)]
+
+
+def norm_into(out, start, source, gain, count):
+    for span in pieces(count, 64):
+        out[start + span.start : start + span.stop, :] = norm_rows(
+            source[span, :].astype(F32), gain
+        )
+
+
+def bring(source, target, sem):
+    copy = pltpu.make_async_copy(source, target, sem)
+    copy.start()
+    return copy
+
+
+def pick_matrix(offsets, heads, groups, stride):
+    count = groups * stride
+    place = lax.broadcasted_iota(jnp.int32, (groups, count), 1)
+    place = place - lax.broadcasted_iota(jnp.int32, (groups, count), 0) * stride
+    return jnp.concatenate([one_hot(place == offsets[h]) for h in range(heads)], axis=0)
+
+
+def project_keys(chosen, heads, weights, keyval_ref):
+    rows, width = chosen.shape
+    groups, head_size = rows // heads, width // heads
+    column = lax.broadcasted_iota(jnp.int32, (groups, width), 1)
+    for slot, weight in enumerate(weights):
+        wide = dot(chosen, weight())
+        total = jnp.zeros((groups, width), F32)
+        for h in range(heads):
+            own = (column >= h * head_size) & (column < (h + 1) * head_size)
+            total = jnp.where(own, wide[h * groups : (h + 1) * groups], total)
+        total = total.astype(BF16)
+        for copy in range(keyval_ref.shape[0]):
+            keyval_ref[copy, slot] = total
+
+
+def ranks(offsets, chunk, stride, share, axis):
+    heads = offsets.shape[0]
+
+    def places(way):
+        shape = (1, chunk) if way else (chunk, 1)
+        place = lax.broadcasted_iota(jnp.int32, shape, way)
+        inside = lax.rem(place, stride)
+        taken = inside == offsets[0]
+        for h in range(1, heads):
+            taken = taken | (inside == offsets[h])
+        return place, inside, jnp.where(taken, inside, inside + stride)
+
+    place, inside, order = places(axis)
+    other_place, _, other_order = places(1 - axis)
+    ahead = (other_order < order) & (lax.div(other_place, stride) == lax.div(place, stride))
+    rank = jnp.sum(jnp.where(ahead, 1, 0), axis=1 - axis, keepdims=True)
+    group = lax.div(place, stride)
+    return jnp.where(
+        rank < heads, group * heads + rank, share + group * (stride - heads) + rank - heads
+    )
+
+
+def slots_of(offsets, heads):
+    values = [offsets[h] for h in range(heads)]
+    fresh = []
+    for h in range(heads):
+        seen = jnp.int32(1)
+        for earlier in values[:h]:
+            seen = jnp.where(earlier == values[h], 0, seen)
+        fresh.append(seen)
+    slots = []
+    for h in range(heads):
+        slot = jnp.int32(0)
+        for other in range(heads):
+            slot = slot + jnp.where(values[other] < values[h], fresh[other], 0)
+        slots.append(slot)
+    return slots
+
+
+def first_keys_kernel(
+    offsets, tokens, gain, key_weight, value_weight, keyval, rows, wide, sems, *, stride
+):
+    copies = [
+        bring(tokens, rows, sems.at[0]),
+        bring(key_weight, wide.at[0], sems.at[1]),
+        bring(value_weight, wide.at[1], sems.at[2]),
+    ]
+    heads = offsets.shape[0]
+    chooser = pick_matrix(offsets, heads, rows.shape[0] // stride, stride)
+    copies[0].wait()
+    chosen = norm_rows(dot(chooser, rows[...]), gain[...])
+
+    def weight(slot):
+        copies[slot + 1].wait()
+        return wide[slot]
+
+    project_keys(
+        chosen, heads, [functools.partial(weight, slot) for slot in range(2)], keyval
+    )
+
+
+def first_query_kernel(
+    offsets, tokens, gain, weight, moved_rows, query, rows, held, normed, sems, *, stride, chunk
+):
+    copies = [bring(tokens, rows, sems.at[0]), bring(weight, held, sems.at[1])]
+    count = tokens.shape[0]
+    share = chunk // stride * offsets.shape[0]
+    rest = chunk - share
+    picked = count // chunk * share
+    mover = one_hot(
+        lax.broadcasted_iota(jnp.int32, (chunk, chunk), 0)
+        == ranks(offsets, chunk, stride, share, 1)
+    )
+    copies[0].wait()
+    for c in range(count // chunk):
+        moved = dot(mover, rows[c * chunk : (c + 1) * chunk, :]).astype(BF16)
+        moved_rows[c * share : (c + 1) * share, :] = moved[:share]
+        moved_rows[picked + c * rest : picked + (c + 1) * rest, :] = moved[share:]
+    norm_into(normed, 0, moved_rows, gain[...], count)
+    copies[1].wait()
+    for span in pieces(count, 512):
+        query[span, :] = dot(normed[span, :], held[...]).astype(BF16)
+
+
+def head_windows(head_size, width):
+    period = min(width, math.lcm(head_size, 128))
+    windows = []
+    for h in range(period // head_size):
+        start = h * head_size // 128 * 128
+        stop = min(period, -(-(h + 1) * head_size // 128) * 128)
+        windows.append((start, stop - start))
+    return period, windows
+
+
+def load_keys(keyvals, heads, keys_ref, values_ref):
+    keys = jnp.concatenate([x[i, 0] for x in keyvals for i in range(x.shape[0])], axis=0)
+    values = jnp.concatenate([x[i, 1] for x in keyvals for i in range(x.shape[0])], axis=0)
+    key_count, width = keys.shape
+    head_size = width // heads
+    period, windows = head_windows(head_size, width)
+    turned = keys.T
+    ones = jnp.ones((key_count, 128), BF16)
+    for h in range(heads):
+        start, size = windows[h % len(windows)]
+        start = start + h // len(windows) * period
+        low = h * head_size - start
+        keys_ref[h, :size, :] = jnp.zeros((size, key_count), BF16)
+        keys_ref[h, low : low + head_size, :] = turned[h * head_size : (h + 1) * head_size]
+        column = lax.broadcasted_iota(jnp.int32, (key_count, size), 1)
+        own = (column >= low) & (column < low + head_size)
+        values_ref[h, :, :size] = jnp.where(
+            own, values[:, start : start + size], jnp.zeros((), BF16)
+        )
+        values_ref[h, :, size : size + 128] = ones
+
+
+def attend_rows(query, first_row, rows, heads, keys_ref, values_ref, mixed_ref, mixed_row, work):
+    scores_ref, weights_ref, sum_ref = work
+    width = query.shape[1]
+    head_size = width // heads
+    period, windows = head_windows(head_size, width)
+    factor = head_size ** (-0.5) * LOG2E
+    span = pl.ds(first_row, rows)
+    out_span = pl.ds(mixed_row, rows)
+
+    @pl.loop(0, width // period)
+    def _(turn):
+        base = pl.multiple_of(turn * period, 128)
+        first = turn * len(windows)
+
+        def score(h):
+            start, size = windows[h]
+            scores_ref[h % 2, :rows] = dot(
+                query[span, pl.ds(base + start, size)], keys_ref[first + h, :size, :]
+            )
+
+        score(0)
+        for h, (start, size) in enumerate(windows):
+            if h + 1 < len(windows):
+                score(h + 1)
+            for part in pieces(rows, 64):
+                scores = scores_ref[h % 2, part, :]
+                highest = jnp.max(scores, axis=1, keepdims=True)
+                weights_ref[h % 2, part, :] = jnp.exp2((scores - highest) * factor).astype(BF16)
+            mixed = dot(weights_ref[h % 2, :rows], values_ref[first + h, :, : size + 128])
+            share = 1.0 / mixed[:, size:]
+            for column in range(0, size, 128):
+                own = mixed[:, column : column + 128] * share
+                at = start + column
+                if h * head_size <= at:
+                    sum_ref[:rows, at : at + 128] = own
+                else:
+                    sum_ref[:rows, at : at + 128] += own
+        mixed_ref[out_span, pl.ds(base, period)] = sum_ref[:rows].astype(BF16)
+
+
+def gelu(x):
+    half = 0.5 * x
+    return half + half * jnp.tanh(x * (0.7978845608028654 + 0.035677408136300125 * (x * x)))
+
+
+def feed_forward(rows, normed, up_weight, down_weight, total, work):
+    wide_ref, inner_ref = work
+    spans = pieces(up_weight.shape[1], wide_ref.shape[2])
+
+    def widen(i):
+        wide_ref[i % 2, :rows] = dot(normed[:rows], up_weight[:, spans[i]])
+
+    widen(0)
+    for i, span in enumerate(spans):
+        if i + 1 < len(spans):
+            widen(i + 1)
+        for part in pieces(rows, 32):
+            inner_ref[i % 2, part, :] = gelu(wide_ref[i % 2, part, :]).astype(BF16)
+        total[:rows] += dot(inner_ref[i % 2, :rows], down_weight[span, :])
+
+
+def finish_rows(
+    first_row, rows, tokens, mixed, mixed_row, out_weight, gain, up_weight, down_weight, work
+):
+    total, normed, wide_ref, inner_ref = work
+    total[:rows] = (
+        (
+            tokens[pl.ds(first_row, rows), :].astype(F32)
+            + dot(mixed[pl.ds(mixed_row, rows), :], out_weight[...])
+        )
+        .astype(BF16)
+        .astype(F32)
+    )
+    norm_into(normed, 0, total, gain[...], rows)
+    feed_forward(rows, normed, up_weight, down_weight, total, (wide_ref, inner_ref))
+
+
+def picked_kernel(
+    offsets,
+    tokens,
+    query,
+    keyval,
+    keyval_far,
+    out_weight,
+    mlp_gain,
+    up_weight,
+    down_weight,
+    gain,
+    key_weight,
+    value_weight,
+    second,
+    keyval_two,
+    keys_ref,
+    values_ref,
+    held,
+    mixed,
+    scores,
+    weights,
+    sums,
+    total,
+    normed,
+    wide,
+    inner,
+    sems,
+    *,
+    heads,
+):
+    sources = (out_weight, key_weight, value_weight)
+    copies = [bring(x, held.at[i], sems.at[i]) for i, x in enumerate(sources)]
+    rows = second.shape[0]
+    load_keys((keyval, keyval_far), heads, keys_ref, values_ref)
+    attend_rows(
+        query, 0, rows, heads, keys_ref, values_ref, mixed, 0, (scores, weights, sums)
+    )
+    copies[0].wait()
+    finish_rows(
+        0,
+        rows,
+        tokens,
+        mixed,
+        0,
+        held.at[0],
+        mlp_gain,
+        up_weight,
+        down_weight,
+        (total, normed, wide, inner),
+    )
+    second[...] = total[...].astype(BF16)
+    norm_into(normed, 0, second, gain[...], rows)
+    chooser = pick_matrix(slots_of(offsets, heads), heads, rows // heads, heads)
+    chosen = dot(chooser, normed[...]).astype(BF16)
+
+    def weight(slot):
+        copies[slot + 1].wait()
+        return held[slot + 1]
+
+    project_keys(
+        chosen, heads, [functools.partial(weight, slot) for slot in range(2)], keyval_two
+    )
+
+
+def rest_kernel(
+    tokens,
+    query,
+    keys_ref,
+    values_ref,
+    out_weight,
+    mlp_gain,
+    up_weight,
+    down_weight,
+    second,
+    held,
+    mixed,
+    scores,
+    weights,
+    sums,
+    total,
+    normed,
+    wide,
+    inner,
+    sems,
+    *,
+    heads,
+):
+    copy = bring(out_weight, held.at[0], sems.at[0])
+    count = second.shape[0]
+    skip = tokens.shape[0] - count
+    size, block = scores.shape[1], total.shape[0]
+
+    @pl.loop(0, count // size)
+    def _(step):
+        row = pl.multiple_of(step * size, size)
+        attend_rows(
+            query,
+            pl.multiple_of(skip + row, size),
+            size,
+            heads,
+            keys_ref,
+            values_ref,
+            mixed,
+            row,
+            (scores, weights, sums),
+        )
+
+    copy.wait()
+
+    @pl.loop(0, count // block)
+    def _(step):
+        row = pl.multiple_of(step * block, block)
+        finish_rows(
+            pl.multiple_of(skip + row, 16),
+            block,
+            tokens,
+            mixed,
+            row,
+            held.at[0],
+            mlp_gain,
+            up_weight,
+            down_weight,
+            (total, normed, wide, inner),
+        )
+        second[pl.ds(row, block), :] = total[...].astype(BF16)
+
+
+def second_query_kernel(picked, rest, gain, weight, query, held, normed, sems):
+    copy = bring(weight, held.at[0], sems.at[0])
+    norm_into(normed, 0, picked, gain[...], picked.shape[0])
+    norm_into(normed, picked.shape[0], rest, gain[...], rest.shape[0])
+    copy.wait()
+    for span in pieces(query.shape[0], 512):
+        query[span, :] = dot(normed[span, :], held[0]).astype(BF16)
+
+
+def second_kernel(
+    offsets,
+    picked,
+    rest,
+    query,
+    keyval,
+    keyval_far,
+    out_weight,
+    encoded,
+    keys_ref,
+    values_ref,
+    held,
+    mixed,
+    scores,
+    weights,
+    sums,
+    sems,
+    *,
+    heads,
+    stride,
+    chunk,
+):
+    copy = bring(out_weight, held.at[0], sems.at[0])
+    load_keys((keyval, keyval_far), heads, keys_ref, values_ref)
+    count, size = query.shape[0], scores.shape[1]
+
+    @pl.loop(0, count // size)
+    def _(step):
+        row = pl.multiple_of(step * size, size)
+        attend_rows(
+            query,
+            row,
+            size,
+            heads,
+            keys_ref,
+            values_ref,
+            mixed,
+            row,
+            (scores, weights, sums),
+        )
+
+    share = chunk // stride * heads
+    rest_share = chunk - share
+    start = picked.shape[0]
+    back = one_hot(
+        lax.broadcasted_iota(jnp.int32, (chunk, chunk), 1)
+        == ranks(offsets, chunk, stride, share, 0)
+    )
+    copy.wait()
+
+    @pl.loop(0, count // chunk)
+    def _(step):
+        near = pl.multiple_of(step * share, share)
+        far = pl.multiple_of(step * rest_share, rest_share)
+        blend = jnp.concatenate(
+            [
+                mixed[pl.ds(near, share), :],
+                mixed[pl.ds(pl.multiple_of(start + far, 16), rest_share), :],
+            ],
+            axis=0,
+        )
+        rows = jnp.concatenate(
+            [picked[pl.ds(near, share), :], rest[pl.ds(far, rest_share), :]], axis=0
+        )
+        result = (rows.astype(F32) + dot(blend, held[0])).astype(BF16)
+        span = pl.ds(pl.multiple_of(step * chunk, chunk), chunk)
+        encoded[span, :] = dot(back, result).astype(BF16)
+
+
+def local_call(kernel, outs, inputs, scratch, scalars=0, far=(), copies=1, flops=0, name=None):
+    specs, placed = [], []
+    for i, x in enumerate(inputs):
+        if i < scalars:
+            specs.append(pl.BlockSpec(memory_space=pltpu.SMEM))
+        elif i in far:
+            specs.append(pl.BlockSpec(memory_space=pltpu.HBM))
+        else:
+            specs.append(pl.BlockSpec(memory_space=pltpu.VMEM))
+            x = pltpu.with_memory_space_constraint(x, pltpu.VMEM)
+        placed.append(x)
+    return pl.pallas_call(
+        kernel,
+        out_shape=outs,
+        in_specs=specs,
+        out_specs=[pl.BlockSpec(memory_space=pltpu.VMEM)] * len(outs),
+        scratch_shapes=list(scratch) + [pltpu.SemaphoreType.DMA((copies,))],
+        compiler_params=pltpu.CompilerParams(vmem_limit_bytes=VMEM_LIMIT),
+        cost_estimate=pl.CostEstimate(
+            flops=int(flops),
+            transcendentals=0,
+            bytes_accessed=sum(inputs[i].size * inputs[i].dtype.itemsize for i in far),
+        ),
+        name=name,
+    )(*placed)
+
+
+def exchange(keyval, span):
+    size = lax.axis_size("seq")
+    teams = [
+        [start + parity + 2 * i for i in range(span // 2)]
+        for start in range(0, size, span)
+        for parity in range(2)
+    ]
+    near = lax.all_to_all(keyval, "seq", 0, 0, axis_index_groups=teams)
+    return near, swapped(near, "seq", 0)
+
+
+def whole_body(
+    tokens,
+    attn_gain,
+    query_first,
+    key_first,
+    segment_value,
+    output_first,
+    mlp_gain,
+    up_weight,
+    down_weight,
+    second_gain,
+    query_second,
+    key_second,
+    value_second,
+    output_second,
+    segment_offset,
+    global_offset,
+):
+    seq_count = lax.axis_size("seq")
+    seg_span = min(SEG_MAX, seq_count)
+    heads = segment_offset.shape[0]
+    count, width = tokens.shape
+    head_size = width // heads
+    hidden = up_weight.shape[1]
+    stride = count // (KEYS // seg_span)
+    stride_two = count // (KEYS // seq_count)
+    groups, groups_two = count // stride, count // stride_two
+    chunk = max(ROWS, stride_two)
+    picked_count = groups_two * heads
+    rest_count = count - picked_count
+    period, windows = head_windows(head_size, width)
+    window = max(size for _, size in windows)
+    part = hidden // 4 if hidden % 512 == 0 else hidden
+    block = rest_count // 2 if rest_count % 32 == 0 else rest_count
+
+    def near(*shape):
+        return pltpu.VMEM(shape, BF16)
+
+    def attention_work(rows):
+        return [
+            pltpu.VMEM((2, rows, KEYS), F32),
+            pltpu.VMEM((2, rows, KEYS), BF16),
+            pltpu.VMEM((rows, period), F32),
+        ]
+
+    def feed_work(rows):
+        return [
+            pltpu.VMEM((rows, width), F32),
+            pltpu.VMEM((rows, width), BF16),
+            pltpu.VMEM((2, rows, part), F32),
+            pltpu.VMEM((2, rows, part), BF16),
+        ]
+
+    keys_shape, values_shape = near(heads, window, KEYS), near(heads, KEYS, window + 128)
+
+    (keyval,) = local_call(
+        functools.partial(first_keys_kernel, stride=stride),
+        [near(seg_span // 2, 2, groups, width)],
+        (segment_offset, tokens, attn_gain, key_first, segment_value),
+        [near(count, width), near(2, width, width)],
+        scalars=1,
+        far=(1, 3, 4),
+        copies=3,
+        flops=2 * heads * groups * width * (count + 2 * width),
+        name="first_keys",
+    )
+    keyval, keyval_far = exchange(keyval, seg_span)
+    rows, query = local_call(
+        functools.partial(first_query_kernel, stride=stride_two, chunk=chunk),
+        [near(count, width), near(count, width)],
+        (global_offset, tokens, attn_gain, query_first),
+        [near(count, width), near(width, width), near(count, width)],
+        scalars=1,
+        far=(1, 3),
+        copies=2,
+        flops=2 * count * width * (width + chunk),
+        name="first_query",
+    )
+    row_flops = 2 * width * (2 * hidden + width) + 4 * 256 * KEYS * heads
+    picked_second, keyval_two, keys, values = local_call(
+        functools.partial(picked_kernel, heads=heads),
+        [
+            near(picked_count, width),
+            near(seq_count // 2, 2, groups_two, width),
+            keys_shape,
+            values_shape,
+        ],
+        (
+            global_offset,
+            rows,
+            query,
+            keyval,
+            keyval_far,
+            output_first,
+            mlp_gain,
+            up_weight,
+            down_weight,
+            second_gain,
+            key_second,
+            value_second,
+        ),
+        [near(3, width, width), near(picked_count, width)]
+        + attention_work(picked_count)
+        + feed_work(picked_count),
+        scalars=1,
+        far=(5, 10, 11),
+        copies=3,
+        flops=row_flops * picked_count,
+        name="layer_of_picked",
+    )
+    keyval_two, keyval_two_far = exchange(keyval_two, seq_count)
+    (rest_second,) = local_call(
+        functools.partial(rest_kernel, heads=heads),
+        [near(rest_count, width)],
+        (rows, query, keys, values, output_first, mlp_gain, up_weight, down_weight),
+        [near(1, width, width), near(rest_count, width)]
+        + attention_work(math.gcd(rest_count, ROWS))
+        + feed_work(block),
+        far=(4,),
+        flops=row_flops * rest_count,
+        name="layer_of_rest",
+    )
+    (query_two,) = local_call(
+        second_query_kernel,
+        [near(count, width)],
+        (picked_second, rest_second, second_gain, query_second),
+        [near(1, width, width), near(count, width)],
+        far=(3,),
+        flops=2 * count * width * width,
+        name="second_query",
+    )
+    (encoded,) = local_call(
+        functools.partial(second_kernel, heads=heads, stride=stride_two, chunk=chunk),
+        [jax.ShapeDtypeStruct((count, width), BF16)],
+        (
+            global_offset,
+            picked_second,
+            rest_second,
+            query_two,
+            keyval_two,
+            keyval_two_far,
+            output_second,
+        ),
+        [keys_shape, values_shape, near(1, width, width), near(count, width)]
+        + attention_work(math.gcd(count, ROWS)),
+        scalars=1,
+        far=(6,),
+        flops=count * (2 * width * width + 4 * 256 * KEYS * heads),
+        name="second_attention",
+    )
+    return encoded
+
+
 def solution(mesh):
     placed = (
         P(("slides", "seq", "mp"), None),
@@ -166,8 +813,9 @@
         P("mp"),
         P("mp"),
     )
+    fits = mesh.shape["mp"] == 1 and 2 <= mesh.shape["seq"] <= SEG_MAX
     return jax.shard_map(
-        body,
+        whole_body if fits else split_body,
         mesh=mesh,
         in_specs=placed,
         out_specs=P(("slides", "seq", "mp"), None),

time: 133 us -> 100 us (0.75)
  matrix products: 66.8 us -> 0 us
  Pallas kernels: 0 us -> 53.8 us
  waiting for transfers between devices: 17.1 us -> 0.01 us
  blocking collectives: 24.5 us -> 31.1 us
  local copies, waits for them, and re-layouts: 14.6 us -> 10.5 us
  other arithmetic: 3.63 us -> 0 us
  starting transfers between devices: 5.8 us -> 4.24 us
    pallas_call x0 -> x6, Pallas kernels: none -> 53.8 us  [local_call(): pl.pallas_call(kernel, out_shape=outs, in_specs=specs, out_specs=[pl.Bloc...]
    dot_general x13 -> x0, matrix products: 46.7 us -> none  [the longest x1 15.5 us: body(): jnp.dot(inner, down_weight, preferred_element_type=jnp.float32)]
    all_to_all x0 -> x2, blocking collectives: none -> 31.1 us  [exchange(): near = lax.all_to_all(keyval, 'seq', 0, 0, axis_index_groups=teams)]
    all_gather x1 -> x0, blocking collectives: 24.5 us -> none  [spread_global(): keyval_two = lax.all_gather(keyval_two, 'seq', axis=1, tiled=True)]
    sub x2 -> x0, matrix products: 20.1 us -> none  [attend_local(): weights = jnp.exp(scores - highest)]
    ppermute x4 -> x2, waiting for transfers between devices: 17.1 us -> 0.01 us  [swapped(): lax.ppermute(x, axis, [(i, i ^ 1 << apart) for i in range(lax.axis_size(a...]
    reduce_sum x4 -> x0, other arithmetic: 2.1 us -> none  [the longest x3 1.83 us: norm_rows(): spread = jnp.mean(center * center, axis=-1, keepdims=True)]
    unnamed x37 -> x38, local copies, waits for them, and re-layouts: 12.5 us -> 10.5 us
  transfers between devices with their start and end apart: 4 -> 2, of which waited for: 4 -> 0; matrix products, arithmetic and copies ran while one was open for 7% -> 0% of each run, Pallas kernels for 0% -> 25%
where the time goes in v1:
time: 100 us
  Pallas kernels  53.8 us (54%)
  blocking collectives  31.1 us (31%)
  local copies, waits for them, and re-layouts  10.5 us (10%)
  starting transfers between devices  4.24 us (4%)
    pallas_call x6, Pallas kernels, local_call(): pl.pallas_call(kernel, out_shape=outs, in_specs=specs, out_specs=[pl.Bloc...  53.8 us
    all_to_all x2, blocking collectives, exchange(): near = lax.all_to_all(keyval, 'seq', 0, 0, axis_index_groups=teams)  31.1 us
    unnamed x38, local copies, waits for them, and re-layouts  10.5 us
    ppermute x2, starting transfers between devices, swapped(): lax.ppermute(x, axis, [(i, i ^ 1 << apart) for i in range(lax.axis_size(a...  4.24 us
  transfers between devices with their start and end apart: 2, of which 0 were waited for; matrix products, arithmetic and copies ran while one was open for 0% of the time, Pallas kernels for 25%

profile of v1, /device:TPU:1, one launch (start us, length us, event | category | flops | bytes accessed | tf_op | source)
XLA Modules:
  0.0 100.0 jit_solution(8170770693025162113)
XLA Ops:
  0.0 1.4 %copy-done.2 = bf16[1024,768]{1,0:T(8,128)(2,1)S(1)} copy-done((bf16[1024,768]{1,0:T(8,128)(2,1)S(1)}, bf16[1024,768]{1,0:T(8,128)(2,1)}, u32[]{:S(2)}) %copy-start.2) | copy-done | bytes 1572888
  1.4 1.3 %copy-done.8 = bf16[768,768]{1,0:T(8,128)(2,1)S(1)} copy-done((bf16[768,768]{1,0:T(8,128)(2,1)S(1)}, bf16[768,768]{1,0:T(8,128)(2,1)}, u32[]{:S(2)}) %copy-start.8) | copy-done | bytes 1179672
  2.7 1.3 %copy-done.9 = bf16[768,768]{1,0:T(8,128)(2,1)S(1)} copy-done((bf16[768,768]{1,0:T(8,128)(2,1)S(1)}, bf16[768,768]{1,0:T(8,128)(2,1)}, u32[]{:S(2)}) %copy-start.9) | copy-done | bytes 1179672
  4.0 0.7 copy-done.12
  4.6 0.7 copy-done.15
  5.3 3.3 %first_keys.1 = bf16[8,2,16,768]{3,2,1,0:T(8,128)(2,1)S(1)} custom-call(s32[16]{0:T(128)S(1)} %copy-done.15, bf16[1024,768]{1,0:T(8,128)(2,1)S(1)} %copy-done.2, f32[768]{0:T(1024)S(1)} %copy-done.12, bf16[768,768]{1,0:T(8,128)(2,1)S(1)} %copy-done.8, bf16[768,768]{1,0:T(8,128)(2,1)S(1)} %copy-done.9), custom_call_target="tpu_custom_call" | custom-call | flops 1006632960 | bytes 3932160 | tf_op jit(solution)/shard_map/first_keys/pallas_call | solution.py:617
  8.6 16.5 %all_to_all.10.keyval = bf16[8,2,16,768]{3,2,1,0:T(8,128)(2,1)S(1)} all-to-all(bf16[8,2,16,768]{3,2,1,0:T(8,128)(2,1)S(1)} %first_keys.1), channel_id=1, replica_groups={{0,2,4,6,8,10,12,14},{1,3,5,7,9,11,13,15},{16,18,20,22,24,26,28,30},{17..., dimensions={0} | all-to-all | bytes 786432 | tf_op jit(solution)/shard_map/all_to_all | solution.py:640
  25.1 2.7 %collective-permute-start = (bf16[8,2,16,768]{3,2,1,0:T(8,128)(2,1)S(1)}, bf16[8,2,16,768]{3,2,1,0:T(8,128)(2,1)S(1)}, u32[]{:S(2)}, u32[]{:S(2)}) collective-permute-start(bf16[8,2,16,768]{3,2,1,0:T(8,128)(2,1)S(1)} %all_to_all.10.keyval), channel_id=1, source_target_pairs={{0,1},{1,0},{2,3},{3,2},{4,5},{5,4},{6,7},{7,6},{8,9},{9,8},{10,11... | collective-permute-start | bytes 1179656 | tf_op jit(solution)/shard_map/ppermute | solution.py:21
  27.8 0.0 copy-done.13
  27.8 0.0 copy-done.14
  27.8 1.4 %copy-done.3 = bf16[1024,768]{1,0:T(8,128)(2,1)S(1)} copy-done((bf16[1024,768]{1,0:T(8,128)(2,1)S(1)}, bf16[1024,768]{1,0:T(8,128)(2,1)}, u32[]{:S(2)}) %copy-start.3) | copy-done | bytes 1572888
  29.2 1.3 %copy-done.16 = bf16[768,768]{1,0:T(8,128)(2,1)S(1)} copy-done((bf16[768,768]{1,0:T(8,128)(2,1)S(1)}, bf16[768,768]{1,0:T(8,128)(2,1)}, u32[]{:S(2)}) %copy-start.16) | copy-done | bytes 1179672
  30.5 4.0 %first_query.1 = (bf16[1024,768]{1,0:T(8,128)(2,1)S(1)}, bf16[1024,768]{1,0:T(8,128)(2,1)S(1)}) custom-call(s32[16]{0:T(128)S(1)} %copy-done.14, bf16[1024,768]{1,0:T(8,128)(2,1)S(1)} %copy-done.3, f32[768]{0:T(1024)S(1)} %copy-done.13, bf16[768,768]{1,0:T(8,128)(2,1)S(1)} %copy-done.16), custom_call_target="tpu_custom_call" | custom-call | flops 1610612736 | bytes 2752512 | tf_op jit(solution)/shard_map/first_query/pallas_call | solution.py:617
  34.5 0.0 collective-permute-done.keyval_far
  34.5 0.0 copy-done.1
  34.5 0.0 copy-done
  34.5 0.0 copy-done.4
  34.5 0.0 copy-done.10
  34.5 0.0 copy-done.11
  34.5 0.0 copy-start.5
  34.5 1.3 %copy-done.5 = bf16[768,768]{1,0:T(8,128)(2,1)S(1)} copy-done((bf16[768,768]{1,0:T(8,128)(2,1)S(1)}, bf16[768,768]{1,0:T(8,128)(2,1)}, u32[]{:S(2)}) %copy-start.5) | copy-done | bytes 1179672
  35.8 1.3 %copy-done.6 = bf16[768,768]{1,0:T(8,128)(2,1)S(1)} copy-done((bf16[768,768]{1,0:T(8,128)(2,1)S(1)}, bf16[768,768]{1,0:T(8,128)(2,1)}, u32[]{:S(2)}) %copy-start.6) | copy-done | bytes 1179672
  37.1 9.8 %layer_of_picked.1 = (bf16[256,768]{1,0:T(8,128)(2,1)S(1)}, bf16[8,2,16,768]{3,2,1,0:T(8,128)(2,1)S(1)}, bf16[16,256,256]{2,1,0:T(8,128)(2,1)S(1)}, bf16[16,256,384]{2,1,0:T(8,128)(2,1)S(1)}) custom-call(s32[16]{0:T(128)S(1)} %copy-done.14, bf16[1024,768]{1,0:T(8,128)(2,1)S(1)} %get-tuple-element.11.tokens, bf16[1024,768]{1,0:T(8,128)(2,1)S(1)} %get-tuple-element.12.query, ...), custom_call_target="tpu_custom_call" | custom-call | flops 3791650816 | bytes 3538944 | tf_op jit(solution)/shard_map/layer_of_picked/pallas_call | solution.py:617
  46.9 14.7 %all_to_all.11.keyval = bf16[8,2,16,768]{3,2,1,0:T(8,128)(2,1)S(1)} all-to-all(bf16[8,2,16,768]{3,2,1,0:T(8,128)(2,1)S(1)} %get-tuple-element.16), channel_id=1, replica_groups={{0,2,4,6,8,10,12,14},{1,3,5,7,9,11,13,15},{16,18,20,22,24,26,28,30},{17..., dimensions={0} | all-to-all | bytes 786432 | tf_op jit(solution)/shard_map/all_to_all | solution.py:640
  61.5 1.5 %collective-permute-start.1 = (bf16[8,2,16,768]{3,2,1,0:T(8,128)(2,1)S(1)}, bf16[8,2,16,768]{3,2,1,0:T(8,128)(2,1)S(1)}, u32[]{:S(2)}, u32[]{:S(2)}) collective-permute-start(bf16[8,2,16,768]{3,2,1,0:T(8,128)(2,1)S(1)} %all_to_all.11.keyval), channel_id=1, source_target_pairs={{0,1},{1,0},{2,3},{3,2},{4,5},{5,4},{6,7},{7,6},{8,9},{9,8},{10,11... | collective-permute-start | bytes 1179656 | tf_op jit(solution)/shard_map/ppermute | solution.py:21
  63.0 0.0 copy-done.7
  63.0 18.4 %layer_of_rest.1.rest = bf16[768,768]{1,0:T(8,128)(2,1)S(1)} custom-call(bf16[1024,768]{1,0:T(8,128)(2,1)S(1)} %get-tuple-element.11.tokens, bf16[1024,768]{1,0:T(8,128)(2,1)S(1)} %get-tuple-element.12.query, bf16[16,256,256]{2,1,0:T(8,128)(2,1)S(1)} %get-tuple-element.14.keys_ref, bf16[16,256,384]{2,1,0:T(8,128)(2,1)S(1)} %get-tuple-element.15.values_ref, ...), custom_call_target="tpu_custom_call" | custom-call | flops 11374952448 | bytes 1179648 | tf_op jit(solution)/shard_map/layer_of_rest/pallas_call | solution.py:617
  81.4 0.0 copy-done.17
  81.4 0.0 copy-start.18
  81.4 2.9 %second_query.1.query = bf16[1024,768]{1,0:T(8,128)(2,1)S(1)} custom-call(bf16[256,768]{1,0:T(8,128)(2,1)S(1)} %get-tuple-element.13.picked, bf16[768,768]{1,0:T(8,128)(2,1)S(1)} %layer_of_rest.1.rest, f32[768]{0:T(1024)S(1)} %copy-done.11, bf16[768,768]{1,0:T(8,128)(2,1)S(1)} %copy-done.17), custom_call_target="tpu_custom_call" | custom-call | flops 1207959552 | bytes 1179648 | tf_op jit(solution)/shard_map/second_query/pallas_call | solution.py:617
  84.3 0.0 collective-permute-done.1.keyval_far
  84.3 15.6 %second_attention.1 = bf16[1024,768]{1,0:T(8,128)(2,1)} custom-call(s32[16]{0:T(128)S(1)} %copy-done.14, bf16[256,768]{1,0:T(8,128)(2,1)S(1)} %get-tuple-element.13.picked, bf16[768,768]{1,0:T(8,128)(2,1)S(1)} %layer_of_rest.1.rest, bf16[1024,768]{1,0:T(8,128)(2,1)S(1)} %second_query.1.query, bf16[8,2,16,768]{3,2,1,0:T(8,128)(2,1)S(1)} %all_to_all.11.keyval, ...), custom_call_target="tpu_custom_call" | custom-call | flops 5502926848 | bytes 1179648 | tf_op jit(solution)/shard_map/second_attention/pallas_call | solution.py:617
  (18 shorter events, 0.0 us)
Async XLA Ops:
  0.0 1.4 %copy-start.2 = (bf16[1024,768]{1,0:T(8,128)(2,1)S(1)}, bf16[1024,768]{1,0:T(8,128)(2,1)}, u32[]{:S(2)}) copy-start(bf16[1024,768]{1,0:T(8,128)(2,1)} %tokens.3) | copy-start | bytes 4718596
  1.4 1.3 %copy-start.8 = (bf16[768,768]{1,0:T(8,128)(2,1)S(1)}, bf16[768,768]{1,0:T(8,128)(2,1)}, u32[]{:S(2)}) copy-start(bf16[768,768]{1,0:T(8,128)(2,1)} %key_weight.2) | copy-start | bytes 3538948
  2.7 1.3 %copy-start.9 = (bf16[768,768]{1,0:T(8,128)(2,1)S(1)}, bf16[768,768]{1,0:T(8,128)(2,1)}, u32[]{:S(2)}) copy-start(bf16[768,768]{1,0:T(8,128)(2,1)} %value_weight.2) | copy-start | bytes 3538948
  4.0 0.7 copy-start.12
  4.6 0.7 copy-start.15
  5.3 22.5 %copy-start.13 = (f32[768]{0:T(1024)S(1)}, f32[768]{0:T(1024)}, u32[]{:S(2)}) copy-start(f32[768]{0:T(1024)} %gain.5) | copy-start | bytes 9220
  5.3 22.5 %copy-start.14 = (s32[16]{0:T(128)S(1)}, s32[16]{0:T(128)}, u32[]{:S(2)}) copy-start(s32[16]{0:T(128)} %offsets.7) | copy-start | bytes 196
  5.3 29.2 %copy-start.1 = (bf16[3072,768]{1,0:T(8,128)(2,1)S(1)}, bf16[3072,768]{1,0:T(8,128)(2,1)}, u32[]{:S(2)}) copy-start(bf16[3072,768]{1,0:T(8,128)(2,1)} %down_weight.3) | copy-start | bytes 14155780
  25.1 9.4 %copy-start = (bf16[768,3072]{1,0:T(8,128)(2,1)S(1)}, bf16[768,3072]{1,0:T(8,128)(2,1)}, u32[]{:S(2)}) copy-start(bf16[768,3072]{1,0:T(8,128)(2,1)} %up_weight.3) | copy-start | bytes 14155780
  25.1 9.4 %collective-permute-start = (bf16[8,2,16,768]{3,2,1,0:T(8,128)(2,1)S(1)}, bf16[8,2,16,768]{3,2,1,0:T(8,128)(2,1)S(1)}, u32[]{:S(2)}, u32[]{:S(2)}) collective-permute-start(bf16[8,2,16,768]{3,2,1,0:T(8,128)(2,1)S(1)} %all_to_all.10.keyval), channel_id=1, source_target_pairs={{0,1},{1,0},{2,3},{3,2},{4,5},{5,4},{6,7},{7,6},{8,9},{9,8},{10,11... | collective-permute-start | bytes 1179656 | tf_op jit(solution)/shard_map/ppermute | solution.py:21
  27.8 1.4 %copy-start.3 = (bf16[1024,768]{1,0:T(8,128)(2,1)S(1)}, bf16[1024,768]{1,0:T(8,128)(2,1)}, u32[]{:S(2)}) copy-start(bf16[1024,768]{1,0:T(8,128)(2,1)} %tokens.3) | copy-start | bytes 4718596
  29.2 1.3 %copy-start.16 = (bf16[768,768]{1,0:T(8,128)(2,1)S(1)}, bf16[768,768]{1,0:T(8,128)(2,1)}, u32[]{:S(2)}) copy-start(bf16[768,768]{1,0:T(8,128)(2,1)} %weight.2) | copy-start | bytes 3538948
  30.5 4.0 %copy-start.4 = (bf16[768,768]{1,0:T(8,128)(2,1)S(1)}, bf16[768,768]{1,0:T(8,128)(2,1)}, u32[]{:S(2)}) copy-start(bf16[768,768]{1,0:T(8,128)(2,1)} %key_weight.3) | copy-start | bytes 3538948
  30.5 4.0 %copy-start.10 = (f32[768]{0:T(1024)S(1)}, f32[768]{0:T(1024)}, u32[]{:S(2)}) copy-start(f32[768]{0:T(1024)} %mlp_gain.3) | copy-start | bytes 9220
  30.5 4.0 %copy-start.11 = (f32[768]{0:T(1024)S(1)}, f32[768]{0:T(1024)}, u32[]{:S(2)}) copy-start(f32[768]{0:T(1024)} %gain.7) | copy-start | bytes 9220
  34.5 1.3 %copy-start.5 = (bf16[768,768]{1,0:T(8,128)(2,1)S(1)}, bf16[768,768]{1,0:T(8,128)(2,1)}, u32[]{:S(2)}) copy-start(bf16[768,768]{1,0:T(8,128)(2,1)} %value_weight.3) | copy-start | bytes 3538948
  35.8 1.3 %copy-start.6 = (bf16[768,768]{1,0:T(8,128)(2,1)S(1)}, bf16[768,768]{1,0:T(8,128)(2,1)}, u32[]{:S(2)}) copy-start(bf16[768,768]{1,0:T(8,128)(2,1)} %out_weight.4) | copy-start | bytes 3538948
  37.1 26.0 %copy-start.7 = (bf16[768,768]{1,0:T(8,128)(2,1)S(1)}, bf16[768,768]{1,0:T(8,128)(2,1)}, u32[]{:S(2)}) copy-start(bf16[768,768]{1,0:T(8,128)(2,1)} %out_weight.4) | copy-start | bytes 3538948
  61.5 22.8 %collective-permute-start.1 = (bf16[8,2,16,768]{3,2,1,0:T(8,128)(2,1)S(1)}, bf16[8,2,16,768]{3,2,1,0:T(8,128)(2,1)S(1)}, u32[]{:S(2)}, u32[]{:S(2)}) collective-permute-start(bf16[8,2,16,768]{3,2,1,0:T(8,128)(2,1)S(1)} %all_to_all.11.keyval), channel_id=1, source_target_pairs={{0,1},{1,0},{2,3},{3,2},{4,5},{5,4},{6,7},{7,6},{8,9},{9,8},{10,11... | collective-permute-start | bytes 1179656 | tf_op jit(solution)/shard_map/ppermute | solution.py:21
  63.0 18.4 %copy-start.17 = (bf16[768,768]{1,0:T(8,128)(2,1)S(1)}, bf16[768,768]{1,0:T(8,128)(2,1)}, u32[]{:S(2)}) copy-start(bf16[768,768]{1,0:T(8,128)(2,1)} %weight.3) | copy-start | bytes 3538948
  81.4 2.9 %copy-start.18 = (bf16[768,768]{1,0:T(8,128)(2,1)S(1)}, bf16[768,768]{1,0:T(8,128)(2,1)}, u32[]{:S(2)}) copy-start(bf16[768,768]{1,0:T(8,128)(2,1)} %out_weight.5) | copy-start | bytes 3538948
